TPU v7x, 32 devices: a whole 2x2x4 slice. The times are simulated.
32 devices in a mesh: section: 2 (over core), dp: 16 (over z, y, x).
Axes of the slice: x: 2, y: 2, z: 4, core: 2. Of those that a mesh axis runs over, the one named last changes fastest.
Arguments:
- tokens: bfloat16 [32, 160, 768], P('dp'), may hold values from -6 to 6
- lengths: int32 [32], P('dp'), may hold values from 95 to 160, as said below
- cotangent: bfloat16 [32, 160, 768], P('dp'), may hold values from -6 to 6
- w_qkv: bfloat16 [2, 768, 2304], P('section', 'dp'), may hold values from -0.21875 to 0.21875
- w_out: bfloat16 [2, 768, 768], P('section', 'dp'), may hold values from -0.625 to 0.625
- w_up: bfloat16 [2, 768, 3072], P('section', 'dp'), may hold values from -0.21875 to 0.21875
- w_down: bfloat16 [2, 3072, 768], P('section', 'dp'), may hold values from -0.109375 to 0.109375
- vectors: bfloat16 [2, 9216], P('section', 'dp'), may hold values from -1 to 1.75, as said below
Outputs:
- acts: float32 [2, 32, 160, 768], P('section', 'dp')
- grad_in: float32 [2, 32, 160, 768], P('section', 'dp')
- grad_qkv: float32 [2, 768, 2304], P('section', 'dp')
- grad_out: float32 [2, 768, 768], P('section', 'dp')
- grad_up: float32 [2, 768, 3072], P('section', 'dp')
- grad_down: float32 [2, 3072, 768], P('section', 'dp')
- grad_vectors: float32 [2, 9216], P('section', 'dp')
Inputs may be any that keep to these rules, and one draw needn't show every extreme that they name: `lengths`: some chain has exactly 160 residues and some exactly 95. `vectors`: entries 3 * 768 to 3072 and 4608 to 5376 of each layer are norm gains, the others biases.
All inputs are finite; a program needn't handle non-finite values.
Results may differ from a plain program's by a relative error of at most 0.015.
Values may be sent and summed in bfloat16 or wider, within the bound.
No kernel may reach another device: no remote copies, remote signals or barrier semaphores. Data moves between devices by JAX's collectives and lax.ppermute only.
A program may use at most 192 MiB of HBM per device.

v0:
```python
import jax
import jax.numpy as jnp
from jax import lax
from jax.sharding import PartitionSpec as P

HEADS = 12
MICRO = 2


eps_norm = 1e-06
neg_fill = -1000000000.0
root_half = 0.7071067811865476
inv_root_two_pi = 0.3989422804014327


def passed_along(block, axis, distance):
    devices = range(lax.axis_size(axis))
    route = [(i - distance, i) for i in devices if i - distance in devices]
    return lax.ppermute(block, axis, route)


def vector_parts(flat_vec, model_width):
    pieces = [
        flat_vec[position * model_width : (position + 1) * model_width] for position in range(8)
    ]
    pieces.append(flat_vec[8 * model_width :])
    return pieces


def norm_forward(resid, norm_gain, norm_shift):
    row_mean = jnp.mean(resid, axis=-1, keepdims=True)
    centered = resid - row_mean
    variance = jnp.mean(centered * centered, axis=-1, keepdims=True)
    inv_std = lax.rsqrt(variance + eps_norm)
    normed = centered * inv_std
    return (normed * norm_gain + norm_shift, normed, inv_std)


def norm_backward(upstream, normed, inv_std, norm_gain):
    grad_gain = jnp.sum(upstream * normed, axis=0)
    grad_shift = jnp.sum(upstream, axis=0)
    scaled = upstream * norm_gain
    grad_resid = inv_std * (
        scaled
        - jnp.mean(scaled, axis=-1, keepdims=True)
        - normed * jnp.mean(scaled * normed, axis=-1, keepdims=True)
    )
    return (grad_resid, grad_gain, grad_shift)


def attention_scores(q_heads, k_heads, key_valid, score_scale):
    dot_scores = (
        jnp.einsum("bqhe,bkhe->bhqk", q_heads, k_heads, preferred_element_type=jnp.float32)
        * score_scale
    )
    return jnp.where(key_valid[:, None, None, :], dot_scores, neg_fill)


def layer_forward(layer_in, weights, key_valid):
    w_qkv, w_out, w_up, w_down, flat_vec = weights
    chains, length, model_width = layer_in.shape
    bias_q, bias_v, bias_o, gain_one, shift_one, bias_down, gain_two, shift_two, bias_up = (
        vector_parts(flat_vec.astype(jnp.float32), model_width)
    )
    head_size = model_width // HEADS
    score_scale = head_size ** (-0.5)
    flat_rows = layer_in.reshape(-1, model_width)
    rows_low = flat_rows.astype(jnp.bfloat16)
    projected = jnp.dot(rows_low, w_qkv, preferred_element_type=jnp.float32)
    head_shape = (chains, length, HEADS, head_size)
    queries = (projected[:, :model_width] + bias_q).astype(jnp.bfloat16).reshape(head_shape)
    keys_low = projected[:, model_width : 2 * model_width].astype(jnp.bfloat16).reshape(head_shape)
    values = (projected[:, 2 * model_width :] + bias_v).astype(jnp.bfloat16).reshape(head_shape)
    scores = attention_scores(queries, keys_low, key_valid, score_scale)
    row_max = jnp.max(scores, axis=-1, keepdims=True)
    shifted_exp = jnp.exp(scores - row_max)
    row_total = jnp.sum(shifted_exp, axis=-1, keepdims=True)
    soft_low = (shifted_exp / row_total).astype(jnp.bfloat16)
    log_total = row_max + jnp.log(row_total)
    mixed = jnp.einsum("bhqk,bkhe->bqhe", soft_low, values, preferred_element_type=jnp.float32)
    mixed_low = mixed.reshape(-1, model_width).astype(jnp.bfloat16)
    branch = jnp.dot(mixed_low, w_out, preferred_element_type=jnp.float32) + bias_o
    hidden, normed_one, inv_std_one = norm_forward(flat_rows + branch, gain_one, shift_one)
    hidden_low = hidden.astype(jnp.bfloat16)
    pre_act = jnp.dot(hidden_low, w_up, preferred_element_type=jnp.float32) + bias_up
    act_low = jax.nn.gelu(pre_act, approximate=False).astype(jnp.bfloat16)
    branch_ff = jnp.dot(act_low, w_down, preferred_element_type=jnp.float32) + bias_down
    result, normed_two, inv_std_two = norm_forward(hidden + branch_ff, gain_two, shift_two)
    stored = (
        rows_low,
        queries,
        keys_low,
        values,
        log_total,
        mixed_low,
        normed_one,
        inv_std_one,
        hidden_low,
        pre_act,
        act_low,
        normed_two,
        inv_std_two,
    )
    return (result.reshape(layer_in.shape), stored)


def layer_backward(upstream, stored, weights, key_valid):
    w_qkv, w_out, w_up, w_down, flat_vec = weights
    (
        rows_low,
        queries,
        keys_low,
        values,
        log_total,
        mixed_low,
        normed_one,
        inv_std_one,
        hidden_low,
        pre_act,
        act_low,
        normed_two,
        inv_std_two,
    ) = stored
    chains, length, model_width = upstream.shape
    parts = vector_parts(flat_vec.astype(jnp.float32), model_width)
    gain_one, gain_two = (parts[3], parts[6])
    head_size = model_width // HEADS
    score_scale = head_size ** (-0.5)
    flat_grad = upstream.reshape(-1, model_width)
    grad_resid_two, grad_gain_two, grad_shift_two = norm_backward(
        flat_grad, normed_two, inv_std_two, gain_two
    )
    grad_ff_low = grad_resid_two.astype(jnp.bfloat16)
    grad_bias_down = jnp.sum(grad_ff_low, axis=0, dtype=jnp.float32)
    grad_w_down = jnp.einsum("rf,rd->fd", act_low, grad_ff_low, preferred_element_type=jnp.float32)
    grad_act = jnp.einsum("rd,fd->rf", grad_ff_low, w_down, preferred_element_type=jnp.float32)
    cdf_part = 0.5 * (1.0 + lax.erf(pre_act * root_half))
    pdf_part = pre_act * inv_root_two_pi * jnp.exp(-0.5 * pre_act * pre_act)
    grad_pre_low = (grad_act * (cdf_part + pdf_part)).astype(jnp.bfloat16)
    grad_bias_up = jnp.sum(grad_pre_low, axis=0, dtype=jnp.float32)
    grad_w_up = jnp.einsum(
        "rd,rf->df", hidden_low, grad_pre_low, preferred_element_type=jnp.float32
    )
    grad_hidden = grad_resid_two + jnp.einsum(
        "rf,df->rd", grad_pre_low, w_up, preferred_element_type=jnp.float32
    )
    grad_resid_one, grad_gain_one, grad_shift_one = norm_backward(
        grad_hidden, normed_one, inv_std_one, gain_one
    )
    grad_branch_low = grad_resid_one.astype(jnp.bfloat16)
    grad_bias_o = jnp.sum(grad_branch_low, axis=0, dtype=jnp.float32)
    grad_w_out = jnp.einsum(
        "ri,ro->io", mixed_low, grad_branch_low, preferred_element_type=jnp.float32
    )
    grad_mixed = jnp.einsum("ro,io->ri", grad_branch_low, w_out, preferred_element_type=jnp.float32)
    grad_mixed = grad_mixed.astype(jnp.bfloat16).reshape(chains, length, HEADS, head_size)
    scores = attention_scores(queries, keys_low, key_valid, score_scale)
    soft = jnp.exp(scores - log_total)
    grad_soft = jnp.einsum(
        "bqhe,bkhe->bhqk", grad_mixed, values, preferred_element_type=jnp.float32
    )
    grad_values = jnp.einsum(
        "bhqk,bqhe->bkhe", soft.astype(jnp.bfloat16), grad_mixed, preferred_element_type=jnp.float32
    )
    row_dot = jnp.sum(soft * grad_soft, axis=-1, keepdims=True)
    grad_scores = (soft * (grad_soft - row_dot)).astype(jnp.bfloat16)
    grad_queries = (
        jnp.einsum("bhqk,bkhe->bqhe", grad_scores, keys_low, preferred_element_type=jnp.float32)
        * score_scale
    )
    grad_keys = (
        jnp.einsum("bhqk,bqhe->bkhe", grad_scores, queries, preferred_element_type=jnp.float32)
        * score_scale
    )
    flat_shape = (-1, model_width)
    grad_q_low = grad_queries.reshape(flat_shape).astype(jnp.bfloat16)
    grad_k_low = grad_keys.reshape(flat_shape).astype(jnp.bfloat16)
    grad_v_low = grad_values.reshape(flat_shape).astype(jnp.bfloat16)
    grad_proj = jnp.concatenate([grad_q_low, grad_k_low, grad_v_low], axis=1)
    grad_w_qkv = jnp.einsum("rd,rc->dc", rows_low, grad_proj, preferred_element_type=jnp.float32)
    grad_layer_in = grad_resid_one + jnp.einsum(
        "rc,dc->rd", grad_proj, w_qkv, preferred_element_type=jnp.float32
    )
    grad_bias_q = jnp.sum(grad_q_low, axis=0, dtype=jnp.float32)
    grad_bias_v = jnp.sum(grad_v_low, axis=0, dtype=jnp.float32)
    grad_vec = jnp.concatenate(
        [
            grad_bias_q,
            grad_bias_v,
            grad_bias_o,
            grad_gain_one,
            grad_shift_one,
            grad_bias_down,
            grad_gain_two,
            grad_shift_two,
            grad_bias_up,
        ]
    )
    return (
        grad_layer_in.reshape(upstream.shape),
        (grad_w_qkv, grad_w_out, grad_w_up, grad_w_down, grad_vec),
    )


def body(tokens, lengths, cotangent, w_qkv, w_out, w_up, w_down, vectors):
    section_index = lax.axis_index("section")
    is_first = section_index == 0
    shards = (w_qkv[0], w_out[0], w_up[0], w_down[0], vectors[0])
    weights = (
        lax.all_gather(w_qkv[0], "dp", axis=0, tiled=True),
        lax.all_gather(w_out[0], "dp", axis=0, tiled=True),
        lax.all_gather(w_up[0], "dp", axis=0, tiled=True),
        lax.all_gather(w_down[0], "dp", axis=0, tiled=True),
        lax.all_gather(vectors[0], "dp", axis=0, tiled=True),
    )
    chains_dev, length, model_width = tokens.shape
    chains_mb = chains_dev // MICRO
    tok_mb = tokens.reshape(MICRO, chains_mb, length, model_width)
    cot_mb = cotangent.reshape(MICRO, chains_mb, length, model_width)
    lengths_mb = lengths.reshape(MICRO, chains_mb)
    positions = jnp.arange(length)

    def mask_for(slot_index):
        chosen = lax.dynamic_index_in_dim(lengths_mb, slot_index, 0, keepdims=False)
        return positions[None, :] < chosen[:, None]

    received = jnp.zeros((chains_mb, length, model_width), jnp.bfloat16)
    stored_list = []
    result_list = []
    for moment in range(MICRO + 1):
        slot_index = jnp.clip(moment - section_index, 0, MICRO - 1)
        key_valid = mask_for(slot_index)
        local_in = tok_mb[min(moment, MICRO - 1)]
        layer_in = jnp.where(is_first, local_in, received).astype(jnp.float32)
        result, stored = layer_forward(layer_in, weights, key_valid)
        result_list.append(result)
        stored_list.append(stored)
        if moment < MICRO:
            received = passed_along(result.astype(jnp.bfloat16), "section", 1)
    acts_local = jnp.stack(
        [
            jnp.where(is_first, result_list[batch_slot], result_list[batch_slot + 1])
            for batch_slot in range(MICRO)
        ]
    )
    weights = (
        lax.all_gather(shards[0], "dp", axis=0, tiled=True),
        lax.all_gather(shards[1], "dp", axis=0, tiled=True),
        lax.all_gather(shards[2], "dp", axis=0, tiled=True),
        lax.all_gather(shards[3], "dp", axis=0, tiled=True),
        lax.all_gather(shards[4], "dp", axis=0, tiled=True),
    )
    totals = tuple((jnp.zeros(tensor.shape, jnp.float32) for tensor in weights))
    summed = tuple((jnp.zeros(tensor.shape, jnp.float32) for tensor in shards))
    received_grad = jnp.zeros((chains_mb, length, model_width), jnp.bfloat16)
    grad_list = []
    for moment in range(MICRO + 1):
        slot_index = jnp.clip(moment - 1 + section_index, 0, MICRO - 1)
        key_valid = mask_for(slot_index)
        stored = jax.tree.map(
            lambda left, right: jnp.where(is_first, left, right),
            stored_list[max(moment - 1, 0)],
            stored_list[min(moment + 1, MICRO)],
        )
        local_grad = jnp.where(
            key_valid[..., None], cot_mb[min(moment, MICRO - 1)].astype(jnp.float32), 0.0
        )
        upstream = jnp.where(is_first, received_grad.astype(jnp.float32), local_grad)
        grad_layer_in, grads = layer_backward(upstream, stored, weights, key_valid)
        is_live = jnp.where(is_first, moment >= 1, moment < MICRO)
        grad_list.append(grad_layer_in)
        if moment < MICRO:
            received_grad = passed_along(grad_layer_in.astype(jnp.bfloat16), "section", -1)
        totals = tuple(
            (jnp.where(is_live, total + grad, total) for total, grad in zip(totals, grads))
        )
    grads_local = jnp.stack(
        [
            jnp.where(is_first, grad_list[batch_slot + 1], grad_list[batch_slot])
            for batch_slot in range(MICRO)
        ]
    )
    summed = (
        lax.psum_scatter(totals[0], "dp", scatter_dimension=0, tiled=True),
        lax.psum_scatter(totals[1], "dp", scatter_dimension=0, tiled=True),
        lax.psum_scatter(totals[2], "dp", scatter_dimension=0, tiled=True),
        lax.psum_scatter(totals[3], "dp", scatter_dimension=0, tiled=True),
        lax.psum_scatter(totals[4], "dp", scatter_dimension=0, tiled=True),
    )
    acts_out = acts_local.reshape(chains_dev, length, model_width)[None]
    grad_out_in = grads_local.reshape(chains_dev, length, model_width)[None]
    return (
        acts_out,
        grad_out_in,
        summed[0][None],
        summed[1][None],
        summed[2][None],
        summed[3][None],
        summed[4][None],
    )


def solution(mesh):
    placed = (
        P("dp", None, None),
        P("dp"),
        P("dp", None, None),
        P("section", "dp", None),
        P("section", "dp", None),
        P("section", "dp", None),
        P("section", "dp", None),
        P("section", "dp"),
    )
    return jax.shard_map(
        body,
        mesh=mesh,
        in_specs=placed,
        out_specs=(
            P("section", "dp", None, None),
            P("section", "dp", None, None),
            P("section", "dp", None),
            P("section", "dp", None),
            P("section", "dp", None),
            P("section", "dp", None),
            P("section", "dp"),
        ),
        check_vma=False,
    )
```

profile of v0, /device:TPU:0, one launch (start us, length us, event | category | flops | bytes accessed | tf_op | source)
XLA Modules:
  0.0 1085.2 jit_solution(3001469011270161843)
XLA Ops:
  13.0 79.5 %all-reduce = bf16[9216]{0:T(1024)(128)(2,1)S(1)} all-reduce(bf16[9216]{0:T(1024)(128)(2,1)S(1)} %dynamic-update-slice), channel_id=3, replica_groups=mesh['section'=2,'dp'=16] {'dp'}, use_global_device_ids=true, to_apply=%add | all-reduce | flops 9216 | bytes 36864
  98.4 2.9 fusion.61
  105.1 38.1 %all-gather.12.cloned.1.call-done = bf16[1,768,768]{2,1,0:T(8,128)(2,1)} async-done(((bf16[1,48,768]{2,1,0:T(8,128)(2,1)}), bf16[1,768,768]{2,1,0:T(8,128)(2,1)}) %all-gather.12.cloned.1.call-update) | async-done | bytes 1179664 | tf_op jit(solution)/shard_map/all_gather | solution.py:211
  145.3 80.1 %all-gather.14.cloned.1.call-done = bf16[1,768,3072]{2,1,0:T(8,128)(2,1)} async-done(((bf16[1,48,3072]{2,1,0:T(8,128)(2,1)}), bf16[1,768,3072]{2,1,0:T(8,128)(2,1)}) %all-gather.14.cloned.1.call-update) | async-done | bytes 4718608 | tf_op jit(solution)/shard_map/all_gather | solution.py:212
  225.4 7.8 fusion.65
  233.2 74.0 %all-gather.16.cloned.1.call-done = bf16[1,3072,768]{2,1,0:T(8,128)(2,1)} async-done(((bf16[1,192,768]{2,1,0:T(8,128)(2,1)}), bf16[1,3072,768]{2,1,0:T(8,128)(2,1)}) %all-gather.16.cloned.1.call-update) | async-done | bytes 4718608 | tf_op jit(solution)/shard_map/all_gather | solution.py:213
  307.1 4.0 fusion.280
  334.0 5.1 fusion.68
  346.4 2.6 convert_reduce_fusion.2
  349.0 3.3 multiply_reduce_fusion.5
  385.6 5.9 fusion.71
  403.4 6.4 convert_reduce_fusion.1
  432.6 2.7 convert_reduce_fusion
  441.5 5.6 fusion.188
  447.2 4.1 fusion.187
  461.3 4.3 add_select_fusion.2
  466.3 3.1 fusion.223
  471.1 5.3 add_select_fusion.1
  476.5 3.0 fusion.165
  481.0 5.3 add_select_fusion
  529.1 77.0 %all-reduce.1 = f32[9216]{0:T(1024)} all-reduce(f32[9216]{0:T(1024)} %add_select_fusion.4), channel_id=11, replica_groups=mesh['section'=2,'dp'=16] {'dp'}, use_global_device_ids=true, to_apply=%region_64.65.clone | all-reduce | flops 9216 | bytes 73728
  612.2 112.5 %reduce-scatter.5.cloned.1.call-done = f32[48,2304]{1,0:T(8,128)} async-done(((f32[768,2304]{1,0:T(8,128)}), f32[48,2304]{1,0:T(8,128)}) %reduce-scatter.5.cloned.1.call-update) | async-done | bytes 442384 | tf_op jit(solution)/shard_map/reduce_scatter | solution.py:284
  724.7 177.0 %reduce-scatter.9.cloned.1.call-done = f32[48,3072]{1,0:T(8,128)} async-done(((f32[768,3072]{1,0:T(8,128)}), f32[48,3072]{1,0:T(8,128)}) %reduce-scatter.9.cloned.1.call-update) | async-done | bytes 589840 | tf_op jit(solution)/shard_map/reduce_scatter | solution.py:286
  901.7 176.3 %reduce-scatter.11.cloned.1.call-done = f32[192,768]{1,0:T(8,128)} async-done(((f32[3072,768]{1,0:T(8,128)}), f32[192,768]{1,0:T(8,128)}) %reduce-scatter.11.cloned.1.call-update) | async-done | bytes 589840 | tf_op jit(solution)/shard_map/reduce_scatter | solution.py:287
  (627 shorter events, 180.7 us)
Async XLA Ops:
  7.2 91.2 %all-gather.10.cloned.1.call-start = ((), (), s32[]{:S(2)}) async-start(), calls=%async_computation.8 | async-start | bytes 3760128 | tf_op jit(solution)/shard_map/all_gather | solution.py:210
  7.9 135.3 %all-gather.12.cloned.1.call-start = ((), (), s32[]{:S(2)}) async-start(), calls=%async_computation.9 | async-start | bytes 1253376 | tf_op jit(solution)/shard_map/all_gather | solution.py:211
  8.6 216.7 %all-gather.14.cloned.1.call-start = ((), (), s32[]{:S(2)}) async-start(), calls=%async_computation.10 | async-start | bytes 5013504 | tf_op jit(solution)/shard_map/all_gather | solution.py:212
  9.4 297.8 %all-gather.16.cloned.1.call-start = ((), (), s32[]{:S(2)}) async-start(), calls=%async_computation.11 | async-start | bytes 5013504 | tf_op jit(solution)/shard_map/all_gather | solution.py:213
  10.0 602.2 %reduce-scatter.7.cloned.1.call-start = ((), (), s32[]{:S(2)}) async-start(), calls=%async_computation.5 | async-start | bytes 2506752 | tf_op jit(solution)/shard_map/reduce_scatter | solution.py:285
  103.7 39.5 %copy-start.144 = (f32[768]{0:T(1024)S(1)}, f32[768]{0:T(1024)}, u32[]{:S(2)}) copy-start(f32[768]{0:T(1024)} %get-tuple-element.35) | copy-start | bytes 9220
  105.1 128.1 %copy-start.107 = (bf16[12,64,160]{2,1,0:T(8,128)(2,1)}, bf16[12,64,160]{2,1,0:T(8,128)(2,1)S(1)}, u32[]{:S(2)}) copy-start(bf16[12,64,160]{2,1,0:T(8,128)(2,1)S(1)} %convolution_convert_fusion.5) | copy-start | bytes 737284
  105.1 120.3 %copy-start.163 = (f32[1,3072]{1,0:T(1,128)S(1)}, f32[1,3072]{1,0:T(1,128)}, u32[]{:S(2)}) copy-start(f32[1,3072]{1,0:T(1,128)} %slice.138) | copy-start | bytes 36868
  145.0 88.2 %copy-start.12 = (f32[160,768]{1,0:T(8,128)}, f32[160,768]{1,0:T(8,128)S(1)}, u32[]{:S(2)}) copy-start(f32[160,768]{1,0:T(8,128)S(1)} %get-tuple-element.92) | copy-start | bytes 1474564
  145.0 88.1 %copy-start.127 = (f32[160]{0:T(256)}, f32[160]{0:T(256)S(1)}, u32[]{:S(2)}) copy-start(f32[160]{0:T(256)S(1)} %broadcast_multiply_fusion.17) | copy-start | bytes 1924
  145.2 87.9 %copy-start.170 = (f32[160]{0:T(256)}, f32[160]{0:T(256)S(1)}, u32[]{:S(2)}) copy-start(f32[160]{0:T(256)S(1)} %multiply_reduce_fusion.17) | copy-start | bytes 1924
  145.2 87.9 %copy-start.133 = (f32[160]{0:T(256)}, f32[160]{0:T(256)S(1)}, u32[]{:S(2)}) copy-start(f32[160]{0:T(256)S(1)} %add_rsqrt_fusion.5) | copy-start | bytes 1924
  307.1 14.2 %copy-start = (bf16[1,768,2304]{2,1,0:T(8,128)(2,1)S(1)}, bf16[1,768,2304]{2,1,0:T(8,128)(2,1)}, u32[]{:S(2)}) copy-start(bf16[1,768,2304]{2,1,0:T(8,128)(2,1)} %all-gather.10.cloned.1.call-done) | copy-start | bytes 10616836
  312.7 7.6 collective-permute-start
  333.7 15.3 %copy-start.5 = (f32[160,768]{1,0:T(8,128)}, f32[160,768]{1,0:T(8,128)S(1)}, u32[]{:S(2)}) copy-start(f32[160,768]{1,0:T(8,128)S(1)} %get-tuple-element.100) | copy-start | bytes 1474564
  333.7 15.3 %copy-start.131 = (f32[160]{0:T(256)}, f32[160]{0:T(256)S(1)}, u32[]{:S(2)}) copy-start(f32[160]{0:T(256)S(1)} %broadcast_multiply_fusion.15) | copy-start | bytes 1924
  334.0 15.0 %copy-start.137 = (f32[160]{0:T(256)}, f32[160]{0:T(256)S(1)}, u32[]{:S(2)}) copy-start(f32[160]{0:T(256)S(1)} %add_rsqrt_fusion.3) | copy-start | bytes 1924
  343.1 12.9 %collective-permute-start.1 = (bf16[1,160,768]{2,1,0:T(8,128)(2,1)}, bf16[1,160,768]{2,1,0:T(8,128)(2,1)}, u32[]{:S(2)}, u32[]{:S(2)}) collective-permute-start(bf16[1,160,768]{2,1,0:T(8,128)(2,1)} %get-tuple-element.65), channel_id=1, source_target_pairs={{0,16},{1,17},{2,18},{3,19},{4,20},{5,21},{6,22},{7,23},{8,24},{9,... | collective-permute-start | bytes 737288 | tf_op jit(solution)/shard_map/ppermute | solution.py:19
  384.0 14.9 %collective-permute-start.2 = (bf16[1,160,768]{2,1,0:T(8,128)(2,1)}, bf16[1,160,768]{2,1,0:T(8,128)(2,1)}, u32[]{:S(2)}, u32[]{:S(2)}) collective-permute-start(bf16[1,160,768]{2,1,0:T(8,128)(2,1)} %convert_bitcast_fusion.1), channel_id=1, source_target_pairs={{16,0},{17,1},{18,2},{19,3},{20,4},{21,5},{22,6},{23,7},{24,8},{25... | collective-permute-start | bytes 737288 | tf_op jit(solution)/shard_map/ppermute | solution.py:19
  399.0 10.9 %slice-start.4 = ((s8[4718592]{0:T(1024)(128)(4,1)}), s8[4194304]{0:T(1024)(128)(4,1)S(1)}, s32[]{:S(2)}) async-start(s8[4718592]{0:T(1024)(128)(4,1)} %bitcast.342), calls=%async_computation.16 | async-start | bytes 8388608
  425.2 4.5 collective-permute-start.3
  441.4 283.3 %reduce-scatter.5.cloned.1.call-start = ((), (), s32[]{:S(2)}) async-start(), calls=%async_computation.4 | async-start | bytes 7520256 | tf_op jit(solution)/shard_map/reduce_scatter | solution.py:284
  465.7 436.0 %reduce-scatter.9.cloned.1.call-start = ((), (), s32[]{:S(2)}) async-start(), calls=%async_computation.6 | async-start | bytes 10027008 | tf_op jit(solution)/shard_map/reduce_scatter | solution.py:286
  476.4 601.5 %reduce-scatter.11.cloned.1.call-start = ((), (), s32[]{:S(2)}) async-start(), calls=%async_computation.7 | async-start | bytes 10027008 | tf_op jit(solution)/shard_map/reduce_scatter | solution.py:287
  (200 other events, 601.9 us)
Sparse Core Ops, SparseCore 0:
  10.8 74.4 all-gather.9
  88.1 55.0 all-gather.11
  146.0 79.3 all-gather.13
  228.0 79.0 all-gather.15
  441.5 126.8 reduce-scatter.6
  575.0 149.6 reduce-scatter.4
  731.9 169.7 reduce-scatter.8
  907.9 169.9 reduce-scatter.10
where the time goes:
time: 1090 us
  waiting for transfers between devices  663 us (61%)
  blocking collectives  156 us (14%)
  matrix products  120 us (11%)
  local copies, waits for them, and re-layouts  77.3 us (7%)
  other arithmetic  41.6 us (4%)
  between operations  18.7 us (2%)
    reduce_scatter x1, waiting for transfers between devices, body(): lax.psum_scatter(totals[2], 'dp', scatter_dimension=0, tiled=True)  177 us
    reduce_scatter x1, waiting for transfers between devices, body(): lax.psum_scatter(totals[3], 'dp', scatter_dimension=0, tiled=True)  176 us
    unnamed x2, blocking collectives  156 us
    reduce_scatter x1, waiting for transfers between devices, body(): lax.psum_scatter(totals[0], 'dp', scatter_dimension=0, tiled=True)  113 us
    all_gather x1, waiting for transfers between devices, body(): lax.all_gather(w_up[0], 'dp', axis=0, tiled=True)  80.1 us
    all_gather x1, waiting for transfers between devices, body(): lax.all_gather(w_down[0], 'dp', axis=0, tiled=True)  74 us
    unnamed x452, local copies, waits for them, and re-layouts  41.9 us
    all_gather x1, waiting for transfers between devices, body(): lax.all_gather(w_out[0], 'dp', axis=0, tiled=True)  38.1 us
  transfers between devices with their start and end apart: 12, of which 7 were waited for; matrix products, arithmetic and copies ran while one was open for 13% of the time, Pallas kernels for 0%

commit v1 on v0

v1 whole, which is shorter than its diff:
```python
import functools

import jax
import jax.numpy as jnp
from jax import lax
from jax.experimental import pallas as pl
from jax.experimental.pallas import tpu as pltpu
from jax.sharding import PartitionSpec as P

HEADS = 12
BF = jnp.bfloat16
F32 = jnp.float32
EPS = 1e-06
FILL = -1000000000.0
ROOT_HALF = 0.7071067811865476
INV_ROOT_TWO_PI = 0.3989422804014327
VMEM_BYTES = 40 * 1024 * 1024
ALL = ("section", "dp")


def nn(a, b):
    return lax.dot_general(a, b, (((1,), (0,)), ((), ())), preferred_element_type=F32)


def nt(a, b):
    return lax.dot_general(a, b, (((1,), (1,)), ((), ())), preferred_element_type=F32)


def tn(a, b):
    return lax.dot_general(a, b, (((0,), (0,)), ((), ())), preferred_element_type=F32)


def norm(r, gain, shift):
    mean = jnp.mean(r, axis=-1, keepdims=True)
    cent = r - mean
    inv = lax.rsqrt(jnp.mean(cent * cent, axis=-1, keepdims=True) + EPS)
    n = cent * inv
    return n * gain + shift, n, inv


def norm_back(dy, n, inv, gain):
    t = dy * gain
    dr = inv * (
        t - jnp.mean(t, axis=-1, keepdims=True) - n * jnp.mean(t * n, axis=-1, keepdims=True)
    )
    return dr, jnp.sum(dy * n, axis=0, keepdims=True), jnp.sum(dy, axis=0, keepdims=True)


def span(info, side, slot, blocks, stacked, rows):
    half = info[0] if side == 0 else 1 - info[0]
    owner = info[2 + blocks * side + slot]
    if stacked:
        at = pl.multiple_of(owner * rows, 16)
        return (pl.ds(2 * half, 2), pl.ds(at, rows), slice(None))
    at = pl.multiple_of(owner * (2 * rows) + half * rows, 16)
    return (pl.ds(at, rows), slice(None))


def load_weight(info, parts, dst, sem, stacked):
    if len(parts) == 1:
        copy = pltpu.make_async_copy(parts[0], dst, sem)
        copy.start()
        return copy
    blocks = sum(part.shape[0] for part in parts) // 2
    rows = parts[0].shape[-2]
    slot = 0
    for part in parts:
        for s in range(part.shape[0]):
            side, at = divmod(slot, blocks)
            window = span(info, side, at, blocks, stacked, rows)
            pltpu.make_async_copy(part.at[s], dst.at[window], sem).start()
            slot += 1
    return pltpu.make_async_copy(dst, dst, sem)


def store_grad(info, src, outs, sem, stacked):
    if len(outs) == 1:
        copy = pltpu.make_async_copy(src, outs[0], sem)
        copy.start()
        return copy
    blocks = outs[0].shape[0]
    rows = outs[0].shape[-2]
    for side in (1, 0):
        for s in range(blocks):
            window = span(info, side, s, blocks, stacked, rows)
            pltpu.make_async_copy(src.at[window], outs[side].at[s], sem).start()
    return pltpu.make_async_copy(src, src, sem)


def attention_forward(n_w, info, x, vec, *refs):
    parts, refs = refs[:n_w], refs[n_w:]
    qkv, soft, mixed, hidden, normed, inv, w, sem = refs
    load_weight(info, parts, w, sem, True).wait()
    xb = x[...]
    length, width = xb.shape
    q = (nn(xb, w[0]) + vec[0:1]).astype(BF)
    k = nn(xb, w[1]).astype(BF)
    v = (nn(xb, w[2]) + vec[1:2]).astype(BF)
    qkv[0] = q
    qkv[1] = k
    qkv[2] = v
    size = width // HEADS
    pair = 2 * size
    low_half = lax.broadcasted_iota(jnp.int32, (length, pair), 1) < size
    valid = lax.broadcasted_iota(jnp.int32, (length, length), 1) < info[1]
    for p in range(HEADS // 2):
        at = slice(p * pair, (p + 1) * pair)
        qp, kp, vp = q[:, at], k[:, at], v[:, at]
        sides = []
        for e in range(2):
            qm = jnp.where(low_half if e == 0 else ~low_half, qp, jnp.zeros_like(qp))
            s = jnp.where(valid, nt(qm, kp) * size ** (-0.5), FILL)
            ex = jnp.exp(s - jnp.max(s, axis=-1, keepdims=True))
            a = ex / jnp.sum(ex, axis=-1, keepdims=True)
            soft[2 * p + e] = a
            sides.append(nn(a.astype(BF), vp))
        mixed[:, at] = jnp.where(low_half, sides[0], sides[1]).astype(BF)
    r = xb.astype(F32) + (nn(mixed[...], w[3]) + vec[2:3])
    hidden[...], normed[...], inv[...] = norm(r, vec[3:4], vec[4:5])


def up_forward(n_w, info, hidden, vec, *refs):
    parts, refs = refs[:n_w], refs[n_w:]
    act, slope, w, sem = refs
    load_weight(info, parts, w, sem, True).wait()
    hb = hidden[...].astype(BF)
    for j in range(4):
        u = nn(hb, w[j]) + vec[8 + j : 9 + j]
        cdf = 0.5 * (1.0 + lax.erf(u * ROOT_HALF))
        act[j] = (u * cdf).astype(BF)
        slope[j] = cdf + u * INV_ROOT_TWO_PI * jnp.exp(-0.5 * u * u)


def down_forward(n_w, info, act, hidden, vec, *refs):
    parts, refs = refs[:n_w], refs[n_w:]
    out, normed, inv, w, sem = refs
    load_weight(info, parts, w, sem, False).wait()
    depth = act.shape[2]
    total = nn(act[0], w[:depth])
    for j in range(1, 4):
        total += nn(act[j], w[j * depth : (j + 1) * depth])
    r = hidden[...] + (total + vec[5:6])
    out[...], normed[...], inv[...] = norm(r, vec[6:7], vec[7:8])


def down_backward(first, n_w, n_g, info, dy, normed, inv, act, slope, vec, *refs):
    parts, refs = refs[:n_w], refs[n_w:]
    outs, refs = refs[:n_g], refs[n_g:]
    dr, du, dvec, w, dw, sems = refs
    load = load_weight(info, parts, w, sems.at[0], False)
    g = dy[...].astype(F32)
    if not first:
        rows = lax.broadcasted_iota(jnp.int32, g.shape, 0)
        g = jnp.where(rows < info[1], g, 0.0)
    grad, dgain, dshift = norm_back(g, normed[...], inv[...], vec[6:7])
    dr[...] = grad
    dz = grad.astype(BF)
    dvec[0:1] = jnp.sum(dz.astype(F32), axis=0, keepdims=True)
    dvec[1:2] = dgain
    dvec[2:3] = dshift
    dvec[7:8] = jnp.zeros_like(dshift)
    depth = act.shape[2]
    for j in range(4):
        dw[j * depth : (j + 1) * depth] = tn(act[j], dz).astype(BF)
    store = store_grad(info, dw, outs, sems.at[1], False)
    load.wait()
    for j in range(4):
        back = nt(dz, w[j * depth : (j + 1) * depth])
        low = (back * slope[j]).astype(BF)
        du[j] = low
        dvec[3 + j : 4 + j] = jnp.sum(low.astype(F32), axis=0, keepdims=True)
    store.wait()


def up_backward(n_w, n_g, info, du, dr, hidden, normed, inv, vec, *refs):
    parts, refs = refs[:n_w], refs[n_w:]
    outs, refs = refs[:n_g], refs[n_g:]
    dr1, dvec, w, dw, sems = refs
    load = load_weight(info, parts, w, sems.at[0], True)
    hb = hidden[...].astype(BF)
    for j in range(4):
        dw[j] = tn(hb, du[j]).astype(BF)
    store = store_grad(info, dw, outs, sems.at[1], True)
    load.wait()
    dh = dr[...]
    for j in range(4):
        dh += nt(du[j], w[j])
    grad, dgain, dshift = norm_back(dh, normed[...], inv[...], vec[3:4])
    dr1[...] = grad
    dvec[0:1] = jnp.sum(grad.astype(BF).astype(F32), axis=0, keepdims=True)
    dvec[1:2] = dgain
    dvec[2:3] = dshift
    dvec[3:8] = jnp.zeros((5, dshift.shape[1]), F32)
    store.wait()


def attention_backward(n_w, n_g, info, dr1, x, qkv, soft, mixed, *refs):
    parts, refs = refs[:n_w], refs[n_w:]
    outs, refs = refs[:n_g], refs[n_g:]
    dx, dvec, w, dw, dp, sems = refs
    load = load_weight(info, parts, w, sems.at[0], True)
    db = dr1[...].astype(BF)
    dw[3] = tn(mixed[...], db).astype(BF)
    load.wait()
    do = nt(db, w[3]).astype(BF)
    length, width = do.shape
    size = width // HEADS
    pair = 2 * size
    scale = size ** (-0.5)
    low_half = lax.broadcasted_iota(jnp.int32, (length, pair), 1) < size
    for p in range(HEADS // 2):
        at = slice(p * pair, (p + 1) * pair)
        qp, kp, vp, dop = qkv[0, :, at], qkv[1, :, at], qkv[2, :, at], do[:, at]
        dqs, dks, dvs = [], [], []
        for e in range(2):
            dom = jnp.where(low_half if e == 0 else ~low_half, dop, jnp.zeros_like(dop))
            a = soft[2 * p + e]
            da = nt(dom, vp)
            ds = (a * (da - jnp.sum(a * da, axis=-1, keepdims=True))).astype(BF)
            dvs.append(tn(a.astype(BF), dop))
            dqs.append(nn(ds, kp))
            dks.append(tn(ds, qp))
        dp[0, :, at] = (jnp.where(low_half, dqs[0], dqs[1]) * scale).astype(BF)
        dp[1, :, at] = (jnp.where(low_half, dks[0], dks[1]) * scale).astype(BF)
        dp[2, :, at] = jnp.where(low_half, dvs[0], dvs[1]).astype(BF)
    xb = x[...]
    for j in range(3):
        dw[j] = tn(xb, dp[j]).astype(BF)
    store = store_grad(info, dw, outs, sems.at[1], True)
    total = dr1[...]
    for j in range(3):
        total += nt(dp[j], w[j])
    dx[...] = total
    dvec[0:1] = jnp.sum(dp[0].astype(F32), axis=0, keepdims=True)
    dvec[1:2] = jnp.sum(dp[2].astype(F32), axis=0, keepdims=True)
    dvec[2:8] = jnp.zeros((6, width), F32)
    store.wait()


def call(kernel, info, small, parts, grads, outs, scratch, flops, nbytes):
    vmem = pl.BlockSpec(memory_space=pltpu.VMEM)
    hbm = pl.BlockSpec(memory_space=pl.ANY)
    shapes = [jax.ShapeDtypeStruct(s, BF) for s in grads]
    shapes += [jax.ShapeDtypeStruct(s, d) for s, d in outs]
    return pl.pallas_call(
        kernel,
        out_shape=shapes,
        in_specs=[pl.BlockSpec(memory_space=pltpu.SMEM)]
        + [vmem] * len(small)
        + [hbm] * len(parts),
        out_specs=[hbm] * len(grads) + [vmem] * len(outs),
        scratch_shapes=scratch,
        compiler_params=pltpu.CompilerParams(vmem_limit_bytes=VMEM_BYTES),
        cost_estimate=pl.CostEstimate(flops=flops, bytes_accessed=nbytes, transcendentals=0),
    )(info, *small, *parts)


class Layer:
    def __init__(self, info, vec, length, width):
        self.info, self.vec = info, vec
        self.length, self.width = length, width
        self.row = ((length, width), F32)
        self.col = ((length, 1), F32)
        self.wide = (4, length, width)
        self.size = 2 * length * width * width
        self.stack = pltpu.VMEM((4, width, width), BF)
        self.tall = pltpu.VMEM((4 * width, width), BF)
        self.bytes = 4 * width * width * 2
        self.sem = pltpu.SemaphoreType.DMA
        self.dvec = ((8, width), F32)

    def attention(self, x, parts):
        self.x = x
        low = ((self.length, self.width), BF)
        outs = [((3,) + low[0], BF), ((HEADS, self.length, self.length), F32), low]
        outs += [self.row, self.row, self.col]
        self.qkv, self.soft, self.mixed, self.hidden, self.n1, self.s1 = call(
            functools.partial(attention_forward, len(parts)), self.info, [x, self.vec], parts,
            [], outs, [self.stack, self.sem], 5 * self.size, self.bytes,
        )

    def up(self, parts):
        self.act, self.slope = call(
            functools.partial(up_forward, len(parts)), self.info, [self.hidden, self.vec], parts,
            [], [(self.wide, BF), (self.wide, F32)], [self.stack, self.sem],
            4 * self.size, self.bytes,
        )

    def down(self, parts):
        out, self.n2, self.s2 = call(
            functools.partial(down_forward, len(parts)), self.info,
            [self.act, self.hidden, self.vec], parts,
            [], [self.row, self.row, self.col], [self.tall, self.sem], 4 * self.size, self.bytes,
        )
        return out

    def down_back(self, first, dy, parts, grads):
        got = call(
            functools.partial(down_backward, first, len(parts), len(grads)), self.info,
            [dy, self.n2, self.s2, self.act, self.slope, self.vec], parts, grads,
            [self.row, (self.wide, BF), self.dvec],
            [self.tall, self.tall, self.sem((2,))], 8 * self.size, 2 * self.bytes,
        )
        self.dr, self.du, self.dvec_down = got[len(grads) :]
        return got[: len(grads)]

    def up_back(self, parts, grads):
        got = call(
            functools.partial(up_backward, len(parts), len(grads)), self.info,
            [self.du, self.dr, self.hidden, self.n1, self.s1, self.vec], parts, grads,
            [self.row, self.dvec],
            [self.stack, self.stack, self.sem((2,))], 8 * self.size, 2 * self.bytes,
        )
        self.dr1, self.dvec_up = got[len(grads) :]
        return got[: len(grads)]

    def attention_back(self, parts, grads):
        got = call(
            functools.partial(attention_backward, len(parts), len(grads)), self.info,
            [self.dr1, self.x, self.qkv, self.soft, self.mixed], parts, grads,
            [self.row, self.dvec],
            [self.stack, self.stack, pltpu.VMEM((3, self.length, self.width), BF), self.sem((2,))],
            11 * self.size, 2 * self.bytes,
        )
        self.dx, self.dvec_att = got[len(grads) :]
        return got[: len(grads)]

    def grad_vec(self):
        d, u, a = self.dvec_down, self.dvec_up, self.dvec_att
        return jnp.concatenate([a[0:2], u[0:3], d[0:7]], axis=0)


def route(move):
    size = lax.axis_size("dp")
    pairs = []
    for s in range(2):
        for d in range(size):
            to_s, to_d = move(s, d)
            pairs.append((s * size + d, to_s * size + to_d))
    return pairs


def send(v, pairs):
    return lax.ppermute(v, ALL, pairs)


def after(v, *others):
    return lax.optimization_barrier((v,) + others)[0]


def cube_routes():
    return (
        route(lambda s, d: (s, d ^ 4)),
        route(lambda s, d: (s, d ^ 8)),
        route(lambda s, d: (s, d ^ (1 if s == 0 else 2))),
        route(lambda s, d: (s, d ^ (2 if s == 0 else 1))),
    )


def cube_owners(core, me):
    slot = jnp.arange(16)
    third = jnp.where(core == 0, 1, 2)

    def table(a, b):
        bits = [(slot >> i) & 1 for i in range(4)]
        return me ^ (bits[0] * 4 + bits[1] * 8 + bits[2] * a + bits[3] * b)

    return jnp.concatenate([table(third, 3 - third), table(3 - third, third)]).astype(jnp.int32)


def swap_route():
    return route(lambda s, d: (1 - s, d))


def cube_body(tokens, lengths, cotangent, w_qkv, w_out, w_up, w_down, vectors):
    core = lax.axis_index("section")
    me = lax.axis_index("dp")
    first = core == 0
    _, length, width = tokens.shape
    rows = w_out.shape[1]
    z_low, z_high, third, last = cube_routes()
    swap = swap_route()

    def chunks(w):
        return jnp.stack([w[:, j * width : (j + 1) * width] for j in range(w.shape[1] // width)])

    own = jnp.stack(
        [
            jnp.concatenate([chunks(w_qkv[0]), w_out]),
            chunks(w_up[0]),
            w_down[0].reshape(4, rows, width),
        ]
    )
    mine = lax.dynamic_slice_in_dim(own, 2 * core, 2, 1)
    other = lax.dynamic_slice_in_dim(own, 2 * (1 - core), 2, 1)
    other = send(other, swap)
    zero = jnp.where(first, mine, other)
    one = jnp.where(first, other, mine)
    blocks = [half[p] for half in (zero, one) for p in range(3)]

    vec = jnp.stack([vectors[0], send(vectors[0], swap)])
    vec = jnp.where(first, vec, vec[::-1])[None]
    for bit, pairs in ((0, route(lambda s, d: (s, d ^ 1))), (1, route(lambda s, d: (s, d ^ 2))),
                       (2, z_low), (3, z_high)):
        got = send(vec, pairs)
        upper = (me >> bit) & 1 == 1
        vec = jnp.where(upper, jnp.concatenate([got, vec]), jnp.concatenate([vec, got]))
    vec = vec.transpose(1, 0, 2).reshape(2, -1, width).astype(F32)

    info = jnp.concatenate([core[None], lengths[core][None], cube_owners(core, me)])
    info = info.astype(jnp.int32)
    layers = [Layer(info, vec[l], length, width) for l in range(2)]

    count = len(blocks)
    low, pairs2, high, quads, cross, eights, rest = {}, {}, {}, {}, {}, {}, {}
    swapped, late = {}, {}
    low[0] = send(blocks[0], z_low)
    low[1] = send(blocks[1], z_low)
    pairs2[0] = jnp.stack([blocks[0], low[0]])
    high[0] = send(pairs2[0], z_high)
    for p in range(count):
        quads[p] = jnp.concatenate([pairs2[p], high[p]])
        cross[p] = send(quads[p], third)
        if p + 1 < count:
            pairs2[p + 1] = jnp.stack([blocks[p + 1], low[p + 1]])
            high[p + 1] = send(after(pairs2[p + 1], quads[p]), z_high)
        if p + 2 < count:
            low[p + 2] = send(after(blocks[p + 2], quads[p]), z_low)
        eights[p] = jnp.concatenate([quads[p], cross[p]])
        rest[p] = send(eights[p], last)
        swapped[p] = send(eights[p], swap)
        late[p] = send(rest[p], swap)

    def parts(p):
        got = [eights[p], rest[p], swapped[p], late[p]]
        if p % 3 == 2:
            got = [a.reshape(8, 2 * rows, width) for a in got]
        return got

    x = lax.dynamic_index_in_dim(tokens, core, 0, keepdims=False)
    cot = lax.dynamic_index_in_dim(cotangent, core, 0, keepdims=False)
    results = []
    for l in range(2):
        layer = layers[l]
        layer.attention(x, parts(3 * l))
        layer.up(parts(3 * l + 1))
        y = layer.down(parts(3 * l + 2))
        results.append(y)
        x = y.astype(BF)

    stacked = [(16, 2, rows, width)] * 2
    tall = [(16, 2 * rows, width)] * 2

    def add(a, b):
        return (a.astype(F32) + b.astype(F32)).astype(BF)

    def reduce(keep, give):
        keep = keep.reshape(16, 2, rows, width)
        got = send(give.reshape(16, 2, rows, width), swap)
        for n, pairs in ((8, last), (4, third), (2, z_high), (1, z_low)):
            out = add(keep[n:], got[n:])
            keep = add(keep[:n], got[:n])
            got = send(out, pairs)
        return keep[0].astype(F32) + got[0].astype(F32)

    sums = {}
    dy = cot
    dxs = {}
    for l in (1, 0):
        layer = layers[l]
        sums[l, 2] = reduce(*layer.down_back(l == 0, dy, parts(3 * l + 2), tall))
        sums[l, 1] = reduce(*layer.up_back(parts(3 * l + 1), stacked))
        sums[l, 0] = reduce(*layer.attention_back(parts(3 * l), stacked))
        dxs[l] = layer.dx
        dy = layer.dx.astype(BF)

    def by_layer(a, b):
        keep = jnp.where(first, a, b)
        got = send(jnp.where(first, b, a), swap)
        return keep, got

    def chains(a, b):
        keep, got = by_layer(a, b)
        return jnp.where(first, jnp.stack([keep, got]), jnp.stack([got, keep]))[None]

    acts = chains(*results)
    grads_in = chains(dxs[0], dxs[1])
    whole = []
    for p in range(3):
        keep, got = by_layer(sums[0, p], sums[1, p])
        whole.append(jnp.where(first, jnp.concatenate([keep, got]), jnp.concatenate([got, keep])))

    def side_by_side(stack):
        return jnp.concatenate([stack[j] for j in range(stack.shape[0])], axis=1)[None]

    keep, got = by_layer(layers[0].grad_vec(), layers[1].grad_vec())
    total = (keep + got).reshape(16, -1)
    for bit, pairs in ((3, z_high), (2, z_low), (1, route(lambda s, d: (s, d ^ 2))),
                       (0, route(lambda s, d: (s, d ^ 1)))):
        n = 1 << bit
        mine_at = ((me >> bit) & 1) * n
        give = lax.dynamic_slice_in_dim(total, n - mine_at, n, 0)
        total = lax.dynamic_slice_in_dim(total, mine_at, n, 0) + send(give, pairs)
    return (
        acts,
        grads_in,
        side_by_side(whole[0][:3]),
        whole[0][3][None],
        side_by_side(whole[1]),
        whole[2].reshape(1, 4 * rows, width),
        total,
    )


def plain_body(tokens, lengths, cotangent, w_qkv, w_out, w_up, w_down, vectors):
    core = lax.axis_index("section")
    first = core == 0
    chains_dev, length, width = tokens.shape
    swap = swap_route()
    size = lax.axis_size("dp")
    rows = w_out.shape[1]

    def gathered(w):
        return lax.all_gather(w, "dp", axis=0, tiled=True)

    def both(v):
        got = send(v, swap)
        return jnp.where(first, v, got), jnp.where(first, got, v)

    def chunks(w):
        return jnp.stack([w[:, j * width : (j + 1) * width] for j in range(w.shape[1] // width)])

    att = jnp.concatenate([chunks(gathered(w_qkv[0])), gathered(w_out[0])[None]])
    up = chunks(gathered(w_up[0]))
    down = gathered(w_down[0])
    vec = gathered(vectors[0]).reshape(-1, width).astype(F32)
    att, up, down, vec = both(att), both(up), both(down), both(vec)
    info = jnp.stack([core, lengths[core]]).astype(jnp.int32)
    layers = [Layer(info, vec[l], length, width) for l in range(2)]
    x = lax.dynamic_index_in_dim(tokens, core, 0, keepdims=False)
    dy = lax.dynamic_index_in_dim(cotangent, core, 0, keepdims=False)
    results = []
    for l in range(2):
        layers[l].attention(x, [att[l]])
        layers[l].up([up[l]])
        y = layers[l].down([down[l]])
        results.append(y)
        x = y.astype(BF)
    stacked, tall = [(4, width, width)], [(4 * width, width)]
    grads = {}
    dxs = {}
    for l in (1, 0):
        layer = layers[l]
        (grads[l, 2],) = layer.down_back(l == 0, dy, [down[l]], tall)
        (grads[l, 1],) = layer.up_back([up[l]], stacked)
        (grads[l, 0],) = layer.attention_back([att[l]], stacked)
        dxs[l] = layer.dx
        dy = layer.dx.astype(BF)

    def by_layer(a, b):
        return jnp.where(first, a, b), send(jnp.where(first, b, a), swap)

    def chains(a, b):
        keep, got = by_layer(a, b)
        return jnp.where(first, jnp.stack([keep, got]), jnp.stack([got, keep]))[None]

    def summed(a, b):
        keep, got = by_layer(a, b)
        total = (keep.astype(F32) + got.astype(F32)).astype(keep.dtype)
        dim = total.ndim - 2 if total.ndim > 1 else 0
        got = lax.psum_scatter(total, "dp", scatter_dimension=dim, tiled=True)
        return got.astype(F32)

    def side_by_side(stack):
        return jnp.concatenate([stack[j] for j in range(stack.shape[0])], axis=1)[None]

    g_att = summed(grads[0, 0], grads[1, 0])
    g_up = summed(grads[0, 1], grads[1, 1])
    g_down = summed(grads[0, 2], grads[1, 2])
    g_vec = summed(layers[0].grad_vec().reshape(-1), layers[1].grad_vec().reshape(-1))
    return (
        chains(*results),
        chains(dxs[0], dxs[1]),
        side_by_side(g_att[:3]),
        g_att[3][None],
        side_by_side(g_up),
        g_down[None],
        g_vec[None],
    )


def solution(mesh):
    placed = (
        P("dp", None, None),
        P("dp"),
        P("dp", None, None),
        P("section", "dp", None),
        P("section", "dp", None),
        P("section", "dp", None),
        P("section", "dp", None),
        P("section", "dp"),
    )
    return jax.shard_map(
        cube_body if mesh.shape["dp"] == 16 else plain_body,
        mesh=mesh,
        in_specs=placed,
        out_specs=(
            P("section", "dp", None, None),
            P("section", "dp", None, None),
            P("section", "dp", None),
            P("section", "dp", None),
            P("section", "dp", None),
            P("section", "dp", None),
            P("section", "dp"),
        ),
        check_vma=False,
    )
```

time: 1090 us -> 610 us (0.56)
  waiting for transfers between devices: 663 us -> 328 us
  blocking collectives: 156 us -> 0 us
  matrix products: 120 us -> 0 us
  Pallas kernels: 0 us -> 111 us
  starting transfers between devices: 8.19 us -> 68.4 us
  local copies, waits for them, and re-layouts: 77.3 us -> 54.9 us
  between operations: 18.7 us -> 2.26 us
    reduce_scatter x4 -> x0, waiting for transfers between devices: 466 us -> none  [the longest x1 177 us: body(): lax.psum_scatter(totals[2], 'dp', scatter_dimension=0, tiled=True)]
    ppermute x4 -> x82, waiting for transfers between devices: 2.26 us -> 328 us  [send(): return lax.ppermute(v, ALL, pairs)]
    all_gather x4 -> x0, waiting for transfers between devices: 192 us -> none  [the longest x1 80.1 us: body(): lax.all_gather(w_up[0], 'dp', axis=0, tiled=True)]
    unnamed x2 -> x0, blocking collectives: 156 us -> none
    dot_general x57 -> x0, matrix products: 120 us -> none  [the longest x3 18.8 us: layer_forward(): jnp.dot(hidden_low, w_up, preferred_element_type=jnp.float32) + bias_up]
    pallas_call x0 -> x12, Pallas kernels: none -> 111 us  [call(): pl.pallas_call(kernel, out_shape=shapes, in_specs=[pl.BlockSpec(memory_sp...]
    ppermute x4 -> x82, starting transfers between devices: 7.62 us -> 68.4 us  [send(): return lax.ppermute(v, ALL, pairs)]
    convert_element_type x12 -> x0, local copies, waits for them, and re-layouts: 19 us -> none  [the longest x3 5.62 us: layer_backward(): grad_mixed.astype(jnp.bfloat16).reshape(chains, length, HEADS, head_size)]
  transfers between devices with their start and end apart: 12 -> 82, of which waited for: 7 -> 49; matrix products, arithmetic and copies ran while one was open for 13% -> 6% of each run, Pallas kernels for 0% -> 5%
where the time goes in v1:
time: 610 us; the launch traced here: 600 us
  waiting for transfers between devices  328 us (54%)
  Pallas kernels  111 us (18%)
  starting transfers between devices  68.4 us (11%)
  local copies, waits for them, and re-layouts  54.9 us (9%)
  other arithmetic  35.3 us (6%)
    ppermute x82, waiting for transfers between devices, send(): return lax.ppermute(v, ALL, pairs)  328 us
    pallas_call x12, Pallas kernels, call(): pl.pallas_call(kernel, out_shape=shapes, in_specs=[pl.BlockSpec(memory_sp...  111 us
    ppermute x82, starting transfers between devices, send(): return lax.ppermute(v, ALL, pairs)  68.4 us
    unnamed x202, local copies, waits for them, and re-layouts  48.7 us
    convert_element_type x24, other arithmetic, add(): return (a.astype(F32) + b.astype(F32)).astype(BF)  13.8 us
  transfers between devices with their start and end apart: 82, of which 49 were waited for; matrix products, arithmetic and copies ran while one was open for 6% of the time, Pallas kernels for 5%

profile of v1, /device:TPU:0, one launch (start us, length us, event | category | flops | bytes accessed | tf_op | source)
XLA Modules:
  0.0 600.1 jit_solution(9726371244646824711)
XLA Ops:
  17.5 7.4 %collective-permute-done.12 = bf16[2,48,768]{2,1,0:T(8,128)(2,1)S(1)} collective-permute-done((bf16[2,48,768]{2,1,0:T(8,128)(2,1)S(1)}, bf16[2,48,768]{2,1,0:T(8,128)(2,1)S(1)}, u32[]{:S(2)}, u32[]{:S(2)}) %collective-permute-start.12) | collective-permute-done | bytes 147488 | tf_op jit(solution)/shard_map/ppermute | solution.py:344
  98.9 10.8 %collective-permute-done.4 = bf16[8,2,576]{2,1,0:T(2,128)(2,1)S(1)} collective-permute-done((bf16[8,2,576]{2,1,0:T(2,128)(2,1)S(1)}, bf16[8,2,576]{2,1,0:T(2,128)(2,1)S(1)}, u32[]{:S(2)}, u32[]{:S(2)}) %collective-permute-start.4) | collective-permute-done | bytes 18464 | tf_op jit(solution)/shard_map/ppermute | solution.py:344
  113.6 11.6 %collective-permute-done.20 = bf16[4,2,48,768]{3,2,1,0:T(8,128)(2,1)S(1)} collective-permute-done((bf16[4,2,48,768]{3,2,1,0:T(8,128)(2,1)S(1)}, bf16[4,2,48,768]{3,2,1,0:T(8,128)(2,1)S(1)}, u32[]{:S(2)}, u32[]{:S(2)}) %collective-permute-start.20) | collective-permute-done | bytes 589856 | tf_op jit(solution)/shard_map/ppermute | solution.py:344
  126.7 11.1 %collective-permute-done.26 = bf16[4,2,48,768]{3,2,1,0:T(8,128)(2,1)S(1)} collective-permute-done((bf16[4,2,48,768]{3,2,1,0:T(8,128)(2,1)S(1)}, bf16[4,2,48,768]{3,2,1,0:T(8,128)(2,1)S(1)}, u32[]{:S(2)}, u32[]{:S(2)}) %collective-permute-start.26) | collective-permute-done | bytes 589856 | tf_op jit(solution)/shard_map/ppermute | solution.py:344
  148.2 10.3 %collective-permute-done.38 = bf16[4,2,48,768]{3,2,1,0:T(8,128)(2,1)S(1)} collective-permute-done((bf16[4,2,48,768]{3,2,1,0:T(8,128)(2,1)S(1)}, bf16[4,2,48,768]{3,2,1,0:T(8,128)(2,1)S(1)}, u32[]{:S(2)}, u32[]{:S(2)}) %collective-permute-start.38) | collective-permute-done | bytes 589856 | tf_op jit(solution)/shard_map/ppermute | solution.py:344
  168.3 9.5 %collective-permute-done.27.refs_1_ = bf16[8,2,48,768]{3,2,1,0:T(8,128)(2,1)S(1)} collective-permute-done((bf16[8,2,48,768]{3,2,1,0:T(8,128)(2,1)S(1)}, bf16[8,2,48,768]{3,2,1,0:T(8,128)(2,1)S(1)}, u32[]{:S(2)}, u32[]{:S(2)}) %collective-permute-start.27) | collective-permute-done | bytes 1179680 | tf_op jit(solution)/shard_map/ppermute | solution.py:344
  181.0 9.6 %collective-permute-done.33.refs_1_ = bf16[8,2,48,768]{3,2,1,0:T(8,128)(2,1)} collective-permute-done((bf16[8,2,48,768]{3,2,1,0:T(8,128)(2,1)}, bf16[8,2,48,768]{3,2,1,0:T(8,128)(2,1)}, u32[]{:S(2)}, u32[]{:S(2)}) %collective-permute-start.33) | collective-permute-done | bytes 1179680 | tf_op jit(solution)/shard_map/ppermute | solution.py:344
  190.6 12.6 %collective-permute-done.39 = bf16[8,2,48,768]{3,2,1,0:T(8,128)(2,1)} collective-permute-done((bf16[8,2,48,768]{3,2,1,0:T(8,128)(2,1)}, bf16[8,2,48,768]{3,2,1,0:T(8,128)(2,1)}, u32[]{:S(2)}, u32[]{:S(2)}) %collective-permute-start.39) | collective-permute-done | bytes 1179680 | tf_op jit(solution)/shard_map/ppermute | solution.py:344
  231.7 7.2 %shard_map.138 = (bf16[3,160,768]{2,1,0:T(8,128)(2,1)S(1)}, f32[12,160,160]{2,1,0:T(8,128)S(1)}, bf16[160,768]{1,0:T(8,128)(2,1)S(1)}, f32[160,768]{1,0:T(8,128)...) custom-call(s32[34]{0:T(128)S(1)} %pad_add_fusion.info, bf16[160,768]{1,0:T(8,128)(2,1)S(1)} %convert_element_type.507.x, ...), custom_call_target="tpu_custom_call" | custom-call | flops 943718400 | bytes 4718592 | tf_op jit(solution)/shard_map/pallas_call | solution.py:245
  257.0 9.3 %shard_map.141 = (bf16[16,96,768]{2,1,0:T(8,128)(2,1)S(1)}, bf16[16,96,768]{2,1,0:T(8,128)(2,1)}, f32[160,768]{1,0:T(8,128)S(1)}, bf16[4,160,768]{2,1,0:T(8,128)(2,1)S(1)}, f32[8,768]{1,0:T(8,128)S(1)}) custom-call(s32[34]{0:T(128)S(1)} %pad_add_fusion.info, bf16[160,768]{1,0:T(8,128)(2,1)S(1)} %dynamic-slice_bitcast_fusion.dy, ...), custom_call_target="tpu_custom_call" | custom-call | flops 1509949440 | bytes 9437184 | tf_op jit(solution)/shard_map/pallas_call | solution.py:245
  273.6 7.8 %shard_map.142 = (bf16[16,2,48,768]{3,2,1,0:T(8,128)(2,1)S(1)}, bf16[16,2,48,768]{3,2,1,0:T(8,128)(2,1)S(1)}, f32[160,768]{1,0:T(8,128)S(1)}, f32[8,768]{1,0:T(8,128)S(1)}) custom-call(s32[34]{0:T(128)S(1)} %pad_add_fusion.info, bf16[4,160,768]{2,1,0:T(8,128)(2,1)S(1)} %copy-done.42, f32[160,768]{1,0:T(8,128)S(1)} %copy-done.57, ...), custom_call_target="tpu_custom_call" | custom-call | flops 1509949440 | bytes 9437184 | tf_op jit(solution)/shard_map/pallas_call | solution.py:245
  287.0 25.2 %shard_map.143 = (bf16[16,2,48,768]{3,2,1,0:T(8,128)(2,1)S(1)}, bf16[16,2,48,768]{3,2,1,0:T(8,128)(2,1)S(1)}, f32[160,768]{1,0:T(8,128)S(1)}, f32[8,768]{1,0:T(8,128)S(1)}) custom-call(s32[34]{0:T(128)S(1)} %pad_add_fusion.info, f32[160,768]{1,0:T(8,128)S(1)} %get-tuple-element.86.dr1, bf16[160,768]{1,0:T(8,128)(2,1)S(1)} %convert_element_type.507.x, ...), custom_call_target="tpu_custom_call" | custom-call | flops 2076180480 | bytes 9437184 | tf_op jit(solution)/shard_map/pallas_call | solution.py:245
  316.8 10.9 %shard_map.144 = (bf16[16,96,768]{2,1,0:T(8,128)(2,1)S(1)}, bf16[16,96,768]{2,1,0:T(8,128)(2,1)}, f32[160,768]{1,0:T(8,128)S(1)}, bf16[4,160,768]{2,1,0:T(8,128)(2,1)S(1)}, f32[8,768]{1,0:T(8,128)S(1)}) custom-call(s32[34]{0:T(128)S(1)} %pad_add_fusion.info, bf16[160,768]{1,0:T(8,128)(2,1)S(1)} %convert_element_type.508.dy, f32[160,768]{1,0:T(8,128)S(1)} %copy-done.51, ...), custom_call_target="tpu_custom_call" | custom-call | flops 1509949440 | bytes 9437184 | tf_op jit(solution)/shard_map/pallas_call | solution.py:245
  329.1 9.8 %shard_map.145 = (bf16[16,2,48,768]{3,2,1,0:T(8,128)(2,1)S(1)}, bf16[16,2,48,768]{3,2,1,0:T(8,128)(2,1)S(1)}, f32[160,768]{1,0:T(8,128)S(1)}, f32[8,768]{1,0:T(8,128)S(1)}) custom-call(s32[34]{0:T(128)S(1)} %pad_add_fusion.info, bf16[4,160,768]{2,1,0:T(8,128)(2,1)S(1)} %get-tuple-element.94.du, f32[160,768]{1,0:T(8,128)S(1)} %get-tuple-element.95.dr, ...), custom_call_target="tpu_custom_call" | custom-call | flops 1509949440 | bytes 9437184 | tf_op jit(solution)/shard_map/pallas_call | solution.py:245
  341.8 14.0 %shard_map.146 = (bf16[16,2,48,768]{3,2,1,0:T(8,128)(2,1)S(1)}, bf16[16,2,48,768]{3,2,1,0:T(8,128)(2,1)S(1)}, f32[160,768]{1,0:T(8,128)S(1)}, f32[8,768]{1,0:T(8,128)S(1)}) custom-call(s32[34]{0:T(128)S(1)} %pad_add_fusion.info, f32[160,768]{1,0:T(8,128)S(1)} %get-tuple-element.98.dr1, bf16[160,768]{1,0:T(8,128)(2,1)S(1)} %dynamic-slice_bitcast_fusion.1.x, ...), custom_call_target="tpu_custom_call" | custom-call | flops 2076180480 | bytes 9437184 | tf_op jit(solution)/shard_map/pallas_call | solution.py:245
  409.9 10.8 %collective-permute-done.50 = bf16[8,2,48,768]{3,2,1,0:T(8,128)(2,1)S(1)} collective-permute-done((bf16[8,2,48,768]{3,2,1,0:T(8,128)(2,1)S(1)}, bf16[8,2,48,768]{3,2,1,0:T(8,128)(2,1)S(1)}, u32[]{:S(2)}, u32[]{:S(2)}) %collective-permute-start.50) | collective-permute-done | bytes 1179680 | tf_op jit(solution)/shard_map/ppermute | solution.py:344
  422.5 17.2 %collective-permute-done.56 = bf16[8,2,48,768]{3,2,1,0:T(8,128)(2,1)S(1)} collective-permute-done((bf16[8,2,48,768]{3,2,1,0:T(8,128)(2,1)S(1)}, bf16[8,2,48,768]{3,2,1,0:T(8,128)(2,1)S(1)}, u32[]{:S(2)}, u32[]{:S(2)}) %collective-permute-start.56) | collective-permute-done | bytes 1179680 | tf_op jit(solution)/shard_map/ppermute | solution.py:344
  441.4 17.2 %collective-permute-done.61 = bf16[8,2,48,768]{3,2,1,0:T(8,128)(2,1)S(1)} collective-permute-done((bf16[8,2,48,768]{3,2,1,0:T(8,128)(2,1)S(1)}, bf16[8,2,48,768]{3,2,1,0:T(8,128)(2,1)S(1)}, u32[]{:S(2)}, u32[]{:S(2)}) %collective-permute-start.61) | collective-permute-done | bytes 1179680 | tf_op jit(solution)/shard_map/ppermute | solution.py:344
  460.4 17.2 %collective-permute-done.67 = bf16[8,2,48,768]{3,2,1,0:T(8,128)(2,1)S(1)} collective-permute-done((bf16[8,2,48,768]{3,2,1,0:T(8,128)(2,1)S(1)}, bf16[8,2,48,768]{3,2,1,0:T(8,128)(2,1)S(1)}, u32[]{:S(2)}, u32[]{:S(2)}) %collective-permute-start.67) | collective-permute-done | bytes 1179680 | tf_op jit(solution)/shard_map/ppermute | solution.py:344
  479.3 17.2 %collective-permute-done.72 = bf16[8,2,48,768]{3,2,1,0:T(8,128)(2,1)S(1)} collective-permute-done((bf16[8,2,48,768]{3,2,1,0:T(8,128)(2,1)S(1)}, bf16[8,2,48,768]{3,2,1,0:T(8,128)(2,1)S(1)}, u32[]{:S(2)}, u32[]{:S(2)}) %collective-permute-start.72) | collective-permute-done | bytes 1179680 | tf_op jit(solution)/shard_map/ppermute | solution.py:344
  513.9 25.5 %collective-permute-done.47 = bf16[2,2,48,768]{3,2,1,0:T(8,128)(2,1)S(1)} collective-permute-done((bf16[2,2,48,768]{3,2,1,0:T(8,128)(2,1)S(1)}, bf16[2,2,48,768]{3,2,1,0:T(8,128)(2,1)S(1)}, u32[]{:S(2)}, u32[]{:S(2)}) %collective-permute-start.47) | collective-permute-done | bytes 294944 | tf_op jit(solution)/shard_map/ppermute | solution.py:344
  539.4 12.6 %collective-permute-done.52 = bf16[2,2,48,768]{3,2,1,0:T(8,128)(2,1)S(1)} collective-permute-done((bf16[2,2,48,768]{3,2,1,0:T(8,128)(2,1)S(1)}, bf16[2,2,48,768]{3,2,1,0:T(8,128)(2,1)S(1)}, u32[]{:S(2)}, u32[]{:S(2)}) %collective-permute-start.52) | collective-permute-done | bytes 294944 | tf_op jit(solution)/shard_map/ppermute | solution.py:344
  552.1 6.4 %collective-permute-done.58 = bf16[2,2,48,768]{3,2,1,0:T(8,128)(2,1)S(1)} collective-permute-done((bf16[2,2,48,768]{3,2,1,0:T(8,128)(2,1)S(1)}, bf16[2,2,48,768]{3,2,1,0:T(8,128)(2,1)S(1)}, u32[]{:S(2)}, u32[]{:S(2)}) %collective-permute-start.58) | collective-permute-done | bytes 294944 | tf_op jit(solution)/shard_map/ppermute | solution.py:344
  558.5 6.3 %collective-permute-done.63 = bf16[2,2,48,768]{3,2,1,0:T(8,128)(2,1)S(1)} collective-permute-done((bf16[2,2,48,768]{3,2,1,0:T(8,128)(2,1)S(1)}, bf16[2,2,48,768]{3,2,1,0:T(8,128)(2,1)S(1)}, u32[]{:S(2)}, u32[]{:S(2)}) %collective-permute-start.63) | collective-permute-done | bytes 294944 | tf_op jit(solution)/shard_map/ppermute | solution.py:344
  (456 shorter events, 300.5 us)
Async XLA Ops:
  64.7 32.4 %collective-permute-start.8 = (bf16[4,2,48,768]{3,2,1,0:T(8,128)(2,1)S(1)}, bf16[4,2,48,768]{3,2,1,0:T(8,128)(2,1)}, u32[]{:S(2)}, u32[]{:S(2)}) collective-permute-start(bf16[4,2,48,768]{3,2,1,0:T(8,128)(2,1)S(1)} %pad_maximum_fusion.9), channel_id=1, source_target_pairs={{0,1},{1,0},{2,3},{3,2},{4,5},{5,4},{6,7},{7,6},{8,9},{9,8},{10,11... | collective-permute-start | bytes 1769480 | tf_op jit(solution)/shard_map/ppermute | solution.py:344
  81.2 30.0 %collective-permute-start.14 = (bf16[4,2,48,768]{3,2,1,0:T(8,128)(2,1)}, bf16[4,2,48,768]{3,2,1,0:T(8,128)(2,1)S(1)}, u32[]{:S(2)}, u32[]{:S(2)}) collective-permute-start(bf16[4,2,48,768]{3,2,1,0:T(8,128)(2,1)} %pad_maximum_fusion.10), channel_id=1, source_target_pairs={{0,1},{1,0},{2,3},{3,2},{4,5},{5,4},{6,7},{7,6},{8,9},{9,8},{10,11... | collective-permute-start | bytes 1769480 | tf_op jit(solution)/shard_map/ppermute | solution.py:344
  98.3 41.2 %collective-permute-start.9 = (bf16[8,2,48,768]{3,2,1,0:T(8,128)(2,1)S(1)}, bf16[8,2,48,768]{3,2,1,0:T(8,128)(2,1)}, u32[]{:S(2)}, u32[]{:S(2)}) collective-permute-start(bf16[8,2,48,768]{3,2,1,0:T(8,128)(2,1)S(1)} %pad_maximum_fusion.refs_0_), channel_id=1, source_target_pairs={{0,2},{1,3},{2,0},{3,1},{4,6},{5,7},{6,4},{7,5},{8,10},{9,11},{10,... | collective-permute-start | bytes 3538952 | tf_op jit(solution)/shard_map/ppermute | solution.py:344
  98.9 40.9 %collective-permute-start.10 = (bf16[8,2,48,768]{3,2,1,0:T(8,128)(2,1)S(1)}, bf16[8,2,48,768]{3,2,1,0:T(8,128)(2,1)S(1)}, u32[]{:S(2)}, u32[]{:S(2)}) collective-permute-start(bf16[8,2,48,768]{3,2,1,0:T(8,128)(2,1)S(1)} %pad_maximum_fusion.refs_0_), channel_id=1, source_target_pairs={{0,16},{1,17},{2,18},{3,19},{4,20},{5,21},{6,22},{7,23},{8,24},{9,... | collective-permute-start | bytes 3538952 | tf_op jit(solution)/shard_map/ppermute | solution.py:344
  111.9 48.0 %collective-permute-start.15 = (bf16[8,2,48,768]{3,2,1,0:T(8,128)(2,1)S(1)}, bf16[8,2,48,768]{3,2,1,0:T(8,128)(2,1)}, u32[]{:S(2)}, u32[]{:S(2)}) collective-permute-start(bf16[8,2,48,768]{3,2,1,0:T(8,128)(2,1)S(1)} %pad_maximum_fusion.1.refs_0_), channel_id=1, source_target_pairs={{0,2},{1,3},{2,0},{3,1},{4,6},{5,7},{6,4},{7,5},{8,10},{9,11},{10,... | collective-permute-start | bytes 3538952 | tf_op jit(solution)/shard_map/ppermute | solution.py:344
  166.8 36.4 %collective-permute-start.39 = (bf16[8,2,48,768]{3,2,1,0:T(8,128)(2,1)}, bf16[8,2,48,768]{3,2,1,0:T(8,128)(2,1)}, u32[]{:S(2)}, u32[]{:S(2)}) collective-permute-start(bf16[8,2,48,768]{3,2,1,0:T(8,128)(2,1)} %pad_maximum_fusion.7), channel_id=1, source_target_pairs={{0,2},{1,3},{2,0},{3,1},{4,6},{5,7},{6,4},{7,5},{8,10},{9,11},{10,... | collective-permute-start | bytes 3538952 | tf_op jit(solution)/shard_map/ppermute | solution.py:344
  180.5 51.2 %collective-permute-start.29 = (bf16[8,2,48,768]{3,2,1,0:T(8,128)(2,1)}, bf16[8,2,48,768]{3,2,1,0:T(8,128)(2,1)}, u32[]{:S(2)}, u32[]{:S(2)}) collective-permute-start(bf16[8,2,48,768]{3,2,1,0:T(8,128)(2,1)} %copy-done.8), channel_id=1, source_target_pairs={{0,16},{1,17},{2,18},{3,19},{4,20},{5,21},{6,22},{7,23},{8,24},{9,... | collective-permute-start | bytes 3538952 | tf_op jit(solution)/shard_map/ppermute | solution.py:344
  190.6 52.0 %collective-permute-start.34 = (bf16[8,2,48,768]{3,2,1,0:T(8,128)(2,1)}, bf16[8,2,48,768]{3,2,1,0:T(8,128)(2,1)}, u32[]{:S(2)}, u32[]{:S(2)}) collective-permute-start(bf16[8,2,48,768]{3,2,1,0:T(8,128)(2,1)} %pad_maximum_fusion.5.refs_0_), channel_id=1, source_target_pairs={{0,16},{1,17},{2,18},{3,19},{4,20},{5,21},{6,22},{7,23},{8,24},{9,... | collective-permute-start | bytes 3538952 | tf_op jit(solution)/shard_map/ppermute | solution.py:344
  203.2 44.9 %collective-permute-start.40 = (bf16[8,2,48,768]{3,2,1,0:T(8,128)(2,1)}, bf16[8,2,48,768]{3,2,1,0:T(8,128)(2,1)}, u32[]{:S(2)}, u32[]{:S(2)}) collective-permute-start(bf16[8,2,48,768]{3,2,1,0:T(8,128)(2,1)} %pad_maximum_fusion.7), channel_id=1, source_target_pairs={{0,16},{1,17},{2,18},{3,19},{4,20},{5,21},{6,22},{7,23},{8,24},{9,... | collective-permute-start | bytes 3538952 | tf_op jit(solution)/shard_map/ppermute | solution.py:344
  203.2 39.3 %collective-permute-start.35 = (bf16[8,2,48,768]{3,2,1,0:T(8,128)(2,1)}, bf16[8,2,48,768]{3,2,1,0:T(8,128)(2,1)}, u32[]{:S(2)}, u32[]{:S(2)}) collective-permute-start(bf16[8,2,48,768]{3,2,1,0:T(8,128)(2,1)} %collective-permute-done.33.refs_1_), channel_id=1, source_target_pairs={{0,16},{1,17},{2,18},{3,19},{4,20},{5,21},{6,22},{7,23},{8,24},{9,... | collective-permute-start | bytes 3538952 | tf_op jit(solution)/shard_map/ppermute | solution.py:344
  203.7 44.4 %collective-permute-start.41 = (bf16[8,2,48,768]{3,2,1,0:T(8,128)(2,1)}, bf16[8,2,48,768]{3,2,1,0:T(8,128)(2,1)}, u32[]{:S(2)}, u32[]{:S(2)}) collective-permute-start(bf16[8,2,48,768]{3,2,1,0:T(8,128)(2,1)} %collective-permute-done.39), channel_id=1, source_target_pairs={{0,16},{1,17},{2,18},{3,19},{4,20},{5,21},{6,22},{7,23},{8,24},{9,... | collective-permute-start | bytes 3538952 | tf_op jit(solution)/shard_map/ppermute | solution.py:344
  398.9 40.7 %collective-permute-start.56 = (bf16[8,2,48,768]{3,2,1,0:T(8,128)(2,1)S(1)}, bf16[8,2,48,768]{3,2,1,0:T(8,128)(2,1)S(1)}, u32[]{:S(2)}, u32[]{:S(2)}) collective-permute-start(bf16[8,2,48,768]{3,2,1,0:T(8,128)(2,1)S(1)} %get-tuple-element.126), channel_id=1, source_target_pairs={{0,2},{1,3},{2,0},{3,1},{4,6},{5,7},{6,4},{7,5},{8,10},{9,11},{10,... | collective-permute-start | bytes 3538952 | tf_op jit(solution)/shard_map/ppermute | solution.py:344
  402.9 55.8 %collective-permute-start.61 = (bf16[8,2,48,768]{3,2,1,0:T(8,128)(2,1)S(1)}, bf16[8,2,48,768]{3,2,1,0:T(8,128)(2,1)S(1)}, u32[]{:S(2)}, u32[]{:S(2)}) collective-permute-start(bf16[8,2,48,768]{3,2,1,0:T(8,128)(2,1)S(1)} %get-tuple-element.124), channel_id=1, source_target_pairs={{0,2},{1,3},{2,0},{3,1},{4,6},{5,7},{6,4},{7,5},{8,10},{9,11},{10,... | collective-permute-start | bytes 3538952 | tf_op jit(solution)/shard_map/ppermute | solution.py:344
  404.1 73.5 %collective-permute-start.67 = (bf16[8,2,48,768]{3,2,1,0:T(8,128)(2,1)S(1)}, bf16[8,2,48,768]{3,2,1,0:T(8,128)(2,1)S(1)}, u32[]{:S(2)}, u32[]{:S(2)}) collective-permute-start(bf16[8,2,48,768]{3,2,1,0:T(8,128)(2,1)S(1)} %get-tuple-element.140), channel_id=1, source_target_pairs={{0,2},{1,3},{2,0},{3,1},{4,6},{5,7},{6,4},{7,5},{8,10},{9,11},{10,... | collective-permute-start | bytes 3538952 | tf_op jit(solution)/shard_map/ppermute | solution.py:344
  408.0 88.5 %collective-permute-start.72 = (bf16[8,2,48,768]{3,2,1,0:T(8,128)(2,1)S(1)}, bf16[8,2,48,768]{3,2,1,0:T(8,128)(2,1)S(1)}, u32[]{:S(2)}, u32[]{:S(2)}) collective-permute-start(bf16[8,2,48,768]{3,2,1,0:T(8,128)(2,1)S(1)} %get-tuple-element.134), channel_id=1, source_target_pairs={{0,2},{1,3},{2,0},{3,1},{4,6},{5,7},{6,4},{7,5},{8,10},{9,11},{10,... | collective-permute-start | bytes 3538952 | tf_op jit(solution)/shard_map/ppermute | solution.py:344
  420.7 77.6 %collective-permute-start.46 = (bf16[4,2,48,768]{3,2,1,0:T(8,128)(2,1)S(1)}, bf16[4,2,48,768]{3,2,1,0:T(8,128)(2,1)S(1)}, u32[]{:S(2)}, u32[]{:S(2)}) collective-permute-start(bf16[4,2,48,768]{3,2,1,0:T(8,128)(2,1)S(1)} %get-tuple-element.150), channel_id=1, source_target_pairs={{0,1},{1,0},{2,3},{3,2},{4,5},{5,4},{6,7},{7,6},{8,9},{9,8},{10,11... | collective-permute-start | bytes 1769480 | tf_op jit(solution)/shard_map/ppermute | solution.py:344
  439.6 59.4 %collective-permute-start.51 = (bf16[4,2,48,768]{3,2,1,0:T(8,128)(2,1)S(1)}, bf16[4,2,48,768]{3,2,1,0:T(8,128)(2,1)S(1)}, u32[]{:S(2)}, u32[]{:S(2)}) collective-permute-start(bf16[4,2,48,768]{3,2,1,0:T(8,128)(2,1)S(1)} %get-tuple-element.148), channel_id=1, source_target_pairs={{0,1},{1,0},{2,3},{3,2},{4,5},{5,4},{6,7},{7,6},{8,9},{9,8},{10,11... | collective-permute-start | bytes 1769480 | tf_op jit(solution)/shard_map/ppermute | solution.py:344
  458.6 41.6 %collective-permute-start.57 = (bf16[4,2,48,768]{3,2,1,0:T(8,128)(2,1)S(1)}, bf16[4,2,48,768]{3,2,1,0:T(8,128)(2,1)S(1)}, u32[]{:S(2)}, u32[]{:S(2)}) collective-permute-start(bf16[4,2,48,768]{3,2,1,0:T(8,128)(2,1)S(1)} %get-tuple-element.146), channel_id=1, source_target_pairs={{0,1},{1,0},{2,3},{3,2},{4,5},{5,4},{6,7},{7,6},{8,9},{9,8},{10,11... | collective-permute-start | bytes 1769480 | tf_op jit(solution)/shard_map/ppermute | solution.py:344
  499.1 40.3 %collective-permute-start.47 = (bf16[2,2,48,768]{3,2,1,0:T(8,128)(2,1)S(1)}, bf16[2,2,48,768]{3,2,1,0:T(8,128)(2,1)S(1)}, u32[]{:S(2)}, u32[]{:S(2)}) collective-permute-start(bf16[2,2,48,768]{3,2,1,0:T(8,128)(2,1)S(1)} %get-tuple-element.170), channel_id=1, source_target_pairs={{0,8},{1,9},{2,10},{3,11},{4,12},{5,13},{6,14},{7,15},{8,0},{9,1},... | collective-permute-start | bytes 884744 | tf_op jit(solution)/shard_map/ppermute | solution.py:344
  500.3 51.8 %collective-permute-start.52 = (bf16[2,2,48,768]{3,2,1,0:T(8,128)(2,1)S(1)}, bf16[2,2,48,768]{3,2,1,0:T(8,128)(2,1)S(1)}, u32[]{:S(2)}, u32[]{:S(2)}) collective-permute-start(bf16[2,2,48,768]{3,2,1,0:T(8,128)(2,1)S(1)} %get-tuple-element.168), channel_id=1, source_target_pairs={{0,8},{1,9},{2,10},{3,11},{4,12},{5,13},{6,14},{7,15},{8,0},{9,1},... | collective-permute-start | bytes 884744 | tf_op jit(solution)/shard_map/ppermute | solution.py:344
  502.4 56.0 %collective-permute-start.58 = (bf16[2,2,48,768]{3,2,1,0:T(8,128)(2,1)S(1)}, bf16[2,2,48,768]{3,2,1,0:T(8,128)(2,1)S(1)}, u32[]{:S(2)}, u32[]{:S(2)}) collective-permute-start(bf16[2,2,48,768]{3,2,1,0:T(8,128)(2,1)S(1)} %get-tuple-element.166), channel_id=1, source_target_pairs={{0,8},{1,9},{2,10},{3,11},{4,12},{5,13},{6,14},{7,15},{8,0},{9,1},... | collective-permute-start | bytes 884744 | tf_op jit(solution)/shard_map/ppermute | solution.py:344
  506.4 58.4 %collective-permute-start.63 = (bf16[2,2,48,768]{3,2,1,0:T(8,128)(2,1)S(1)}, bf16[2,2,48,768]{3,2,1,0:T(8,128)(2,1)S(1)}, u32[]{:S(2)}, u32[]{:S(2)}) collective-permute-start(bf16[2,2,48,768]{3,2,1,0:T(8,128)(2,1)S(1)} %get-tuple-element.164), channel_id=1, source_target_pairs={{0,8},{1,9},{2,10},{3,11},{4,12},{5,13},{6,14},{7,15},{8,0},{9,1},... | collective-permute-start | bytes 884744 | tf_op jit(solution)/shard_map/ppermute | solution.py:344
  512.7 58.4 %collective-permute-start.69 = (bf16[2,2,48,768]{3,2,1,0:T(8,128)(2,1)S(1)}, bf16[2,2,48,768]{3,2,1,0:T(8,128)(2,1)S(1)}, u32[]{:S(2)}, u32[]{:S(2)}) collective-permute-start(bf16[2,2,48,768]{3,2,1,0:T(8,128)(2,1)S(1)} %get-tuple-element.162), channel_id=1, source_target_pairs={{0,8},{1,9},{2,10},{3,11},{4,12},{5,13},{6,14},{7,15},{8,0},{9,1},... | collective-permute-start | bytes 884744 | tf_op jit(solution)/shard_map/ppermute | solution.py:344
  539.4 37.9 %collective-permute-start.74 = (bf16[2,2,48,768]{3,2,1,0:T(8,128)(2,1)S(1)}, bf16[2,2,48,768]{3,2,1,0:T(8,128)(2,1)S(1)}, u32[]{:S(2)}, u32[]{:S(2)}) collective-permute-start(bf16[2,2,48,768]{3,2,1,0:T(8,128)(2,1)S(1)} %get-tuple-element.160), channel_id=1, source_target_pairs={{0,8},{1,9},{2,10},{3,11},{4,12},{5,13},{6,14},{7,15},{8,0},{9,1},... | collective-permute-start | bytes 884744 | tf_op jit(solution)/shard_map/ppermute | solution.py:344
  (159 other events, 2108.8 us)
